TPU v7x, 32 devices: a whole 2x2x4 slice. The times are simulated.
32 devices in a mesh: row: 8 (over z, y), col: 4 (over x, core).
Axes of the slice: x: 2, y: 2, z: 4, core: 2. Of those that a mesh axis runs over, the one named last changes fastest.
Arguments:
- similarity: bfloat16 [4096, 4096], P('row', 'col'), may hold values from 0.0009 to 1
- occupancy: int32 [32, 32], P('row', 'col'), may hold values from 0 to 1, as said below
- kept_tiles: int32 [32, 32], P('row', 'col'), may hold values from 0 to 1, as said below
Outputs:
- flow: bfloat16 [4096, 4096], P('row', 'col')
Inputs may be any that keep to these rules, and one draw needn't show every extreme that they name: `occupancy`: 0 or 1; every diagonal tile is 1; the share of ones varies from tile row to tile row. `kept_tiles`: 0 or 1; every diagonal tile is 1; the share of ones varies from tile row to tile row.
All inputs are finite; a program needn't handle non-finite values.
Results may differ from a plain program's by a relative error of at most 0.001.
Values may be sent and summed in bfloat16 or wider, within the bound.
A program may use at most 64 MiB of HBM per device.

v0:
```python
import jax
import jax.numpy as jnp
from jax import lax
from jax.sharding import PartitionSpec as P

TILE = 128
PHASES = 2


def expand_tiles(values, tile_pattern, tile_size):
    rows, cols = values.shape
    shaped = values.reshape(rows // tile_size, tile_size, cols // tile_size, tile_size)
    masked = shaped * tile_pattern.astype(values.dtype)[:, None, :, None]
    return masked.reshape(rows, cols)


def body(similarity, occupancy, kept_tiles):
    local_rows, local_cols = similarity.shape
    order = local_rows * lax.axis_size("row")
    stored = expand_tiles(similarity, occupancy, TILE)
    keep_mask = expand_tiles(jnp.ones((local_rows, local_cols), jnp.float32), kept_tiles, TILE)
    phase_width = local_cols // PHASES
    batches = []
    column_panel = lax.all_gather(stored, "row", axis=0, tiled=True)
    expanded = jnp.dot(
        lax.all_gather(stored, "col", axis=1, tiled=True),
        column_panel,
        preferred_element_type=jnp.float32,
    )
    for phase_index in range(PHASES):
        batches.append(expanded[:, phase_index * phase_width : (phase_index + 1) * phase_width])
    inflated_parts = []
    for phase_index in range(PHASES):
        product = batches[phase_index]
        mask_part = keep_mask[:, phase_index * phase_width : (phase_index + 1) * phase_width]
        inflated_parts.append(product * product * mask_part)
    results = []
    for phase_index in range(PHASES):
        inflated = inflated_parts[phase_index]
        column_total = lax.psum(jnp.sum(inflated, axis=0), "row")
        results.append((order * inflated / column_total[None, :]).astype(jnp.bfloat16))
    return jnp.concatenate(results, axis=1)


def solution(mesh):
    placed = (P("row", "col"), P("row", "col"), P("row", "col"))
    return jax.shard_map(
        body, mesh=mesh, in_specs=placed, out_specs=P("row", "col"), check_vma=False
    )
```

profile of v0, /device:TPU:0, one launch (start us, length us, event | category | flops | bytes accessed | tf_op | source)
XLA Modules:
  0.0 212.2 jit_solution(9801378148829885895)
XLA Ops:
  6.5 0.0 all-gather.3.cloned.1.call-start
  6.5 0.7 convert_element_type.12
  7.2 0.2 mul.34
  7.4 0.0 copy-start.1
  7.4 2.3 %bitcast_multiply_fusion = bf16[512,1024]{1,0:T(8,128)(2,1)} fusion(bf16[512,1024]{1,0:T(8,128)(2,1)} %param.3, bf16[64,8,8,128]{3,2,1,0:T(8,128)(2,1)S(1)} %bitcast.14), kind=kLoop, calls=%fused_computation.1 | loop fusion | flops 524288 | bytes 3145728 | tf_op jit(solution)/shard_map/mul | solution.py:13
  9.8 0.0 all-gather.3.cloned.1.call-update
  9.8 0.0 all-gather.5.cloned.1.call-start
  9.9 0.7 all-gather.5.cloned.1.call-update
  10.6 0.0 copy-done.1
  10.6 0.2 mul.38
  10.8 0.5 copy.8
  11.3 35.9 %all-gather.3.cloned.1.call-done = bf16[512,4096]{1,0:T(8,128)(2,1)} async-done(((bf16[512,1024]{1,0:T(8,128)(2,1)}), bf16[512,4096]{1,0:T(8,128)(2,1)}) %all-gather.3.cloned.1.call-update) | async-done | bytes 4194320 | tf_op jit(solution)/shard_map/all_gather | solution.py:26
  47.1 127.1 %all-gather.5.cloned.1.call-done = bf16[4096,1024]{1,0:T(8,128)(2,1)} async-done(((bf16[512,1024]{1,0:T(8,128)(2,1)}), bf16[4096,1024]{1,0:T(8,128)(2,1)}) %all-gather.5.cloned.1.call-update) | async-done | bytes 8388624 | tf_op jit(solution)/shard_map/all_gather | solution.py:24
  174.2 8.1 %fusion.2 = f32[512,1024]{1,0:T(8,128)S(1)} fusion(bf16[512,4096]{1,0:T(8,128)(2,1)} %all-gather.3.cloned.1.call-done, bf16[4096,1024]{1,0:T(8,128)(2,1)} %all-gather.5.cloned.1.call-done), kind=kOutput, calls=%fused_computation.11 | convolution fusion | flops 4294967296 | bytes 14680064 | tf_op jit(solution)/shard_map/dot_general | solution.py:25
  182.4 0.0 copy-start
  182.4 0.5 fusion
  182.9 0.8 copy-done
  183.7 18.4 %all-reduce = (f32[512]{0:T(512)S(1)}, f32[512]{0:T(512)S(1)}) all-reduce(f32[512]{0:T(512)S(1)} %get-tuple-element.6, f32[512]{0:T(512)S(1)} %get-tuple-element.5), channel_id=1, replica_groups=mesh['row'=8,'col'=4] {'row'}, use_global_device_ids=true, to_apply=%region_3.0 | all-reduce | flops 1024 | bytes 8192 | tf_op jit(solution)/shard_map/psum | solution.py:40
  202.1 2.1 divide_convert_fusion.1
  204.2 1.1 pad_maximum_fusion
  (1 shorter events, 0.0 us)
Async XLA Ops:
  6.5 40.6 %all-gather.3.cloned.1.call-start = ((), (), s32[]{:S(2)}) async-start(), calls=%async_computation | async-start | bytes 5242880 | tf_op jit(solution)/shard_map/all_gather | solution.py:26
  7.4 3.1 %copy-start.1 = (s32[4,8]{1,0:T(4,128)S(1)}, s32[4,8]{1,0:T(4,128)}, u32[]{:S(2)}) copy-start(s32[4,8]{1,0:T(4,128)} %param.5) | copy-start | bytes 388
  9.8 164.4 %all-gather.5.cloned.1.call-start = ((), (), s32[]{:S(2)}) async-start(), calls=%async_computation.1 | async-start | bytes 9437184 | tf_op jit(solution)/shard_map/all_gather | solution.py:24
  182.4 1.3 copy-start
Sparse Core Ops, SparseCore 0:
  9.9 37.1 all-gather.2
  49.3 124.9 all-gather.4
where the time goes:
time: 212 us
  waiting for transfers between devices  164 us (77%)
  blocking collectives  18.4 us (9%)
  between operations  13.5 us (6%)
  matrix products  8.14 us (4%)
  other arithmetic  6.76 us (3%)
    all_gather x1, waiting for transfers between devices, body(): column_panel = lax.all_gather(stored, 'row', axis=0, tiled=True)  127 us
    all_gather x1, waiting for transfers between devices, body(): lax.all_gather(stored, 'col', axis=1, tiled=True)  35.9 us
    psum x1, blocking collectives, body(): column_total = lax.psum(jnp.sum(inflated, axis=0), 'row')  18.4 us
    dot_general x1, matrix products, body(): jnp.dot(lax.all_gather(stored, 'col', axis=1, tiled=True), column_panel,...  8.14 us
  transfers between devices with their start and end apart: 2, of which 2 were waited for; matrix products, arithmetic and copies ran while one was open for 0% of the time, Pallas kernels for 0%

commit v1 on v0

v1 whole, which is shorter than its diff:
```python
import functools

import jax
import jax.numpy as jnp
from jax import lax
from jax.experimental import pallas as pl
from jax.experimental.pallas import tpu as pltpu
from jax.sharding import PartitionSpec as P

TILE = 128
MESH = pl.DeviceIdType.MESH


def kernel(
    nz, nx, nq, order,
    sim, occ, kept, out,
    rp, cp, acc, obuf, tsend, trecv, ksend, kbuf,
    z_send, z_recv, pa_send, pa_recv, yc_send, yc_recv, yf_send, yf_recv,
    yb_send, yb_recv, xo_send, xo_recv, xf_send, xf_recv, xd_send, xd_recv, xg_send, xg_recv,
    t_send, t_recv, o_send, o_recv, k_send, k_recv,
):
    R, W = sim.shape
    H = W // 2
    CW = H // nq
    ir, ic = lax.axis_index("row"), lax.axis_index("col")
    z, y = lax.div(ir, 2), lax.rem(ir, 2)
    x, c = lax.div(ic, 2), lax.rem(ic, 2)
    oy, oc = 1 - y, 1 - c
    home = c == y

    def dev(xx, yy, zz, cc):
        return (zz * 2 + yy, xx * 2 + cc)

    def mult(v, m):
        return pl.multiple_of(v, m)

    def rows(yy):
        return pl.ds(mult(yy * R, R), R)

    def cols(start, width):
        return pl.ds(mult(start, TILE), width)

    def remote(src, dst, ssem, rsem, to):
        return pltpu.make_async_remote_copy(
            src_ref=src, dst_ref=dst, send_sem=ssem, recv_sem=rsem, device_id=to, device_id_type=MESH
        )

    partner = dev(x, y, z, oc)
    across = dev(x, oy, z, c)
    started = []

    def go(copy, cond=None):
        if cond is None:
            copy.start()
        else:
            pl.when(cond)(copy.start)
        started.append((copy, cond))

    barrier = pltpu.get_barrier_semaphore()
    peers = [partner, across, dev(x, oy, z, oc)]
    peers += [dev(lax.rem(x + d, nx), y, z, c) for d in range(1, nx)]
    peers += [dev(x, y, lax.rem(z + d, nz), c) for d in range(1, nz)]
    for peer in peers:
        pl.semaphore_signal(barrier, inc=1, device_id=peer, device_id_type=MESH)

    mycol = (2 * x + c) * W
    for i in range(R // TILE):
        for j in range(W // TILE):
            flag = occ[i, j].astype(jnp.float32)
            tile = sim[i * TILE : (i + 1) * TILE, j * TILE : (j + 1) * TILE].astype(jnp.float32)
            rp[pl.ds(mult(y * R + i * TILE, TILE), TILE), cols(mycol + j * TILE, TILE)] = (tile * flag).astype(
                jnp.bfloat16
            )
    ksend[...] = jnp.zeros_like(ksend)
    for i in range(R // TILE):
        for j in range(W // TILE):
            ksend[i : i + 1, j * TILE : (j + 1) * TILE] = jnp.full(
                (1, TILE), kept[i, j].astype(jnp.float32), jnp.float32
            )
    pl.semaphore_wait(barrier, len(peers))

    mine = rp.at[rows(y), cols(mycol, W)]

    def half_of(yy, start, hh):
        return rp.at[rows(yy), cols(start + hh * H, H)]

    for j, hh in enumerate((oc, c)):
        ref = half_of(y, mycol, hh)
        go(remote(ref, ref, pa_send.at[j], pa_recv.at[j], partner))

    def pa_arrive(j):
        ref = half_of(y, (2 * x + oc) * W, c if j == 0 else oc)
        remote(ref, ref, pa_send.at[j], pa_recv.at[j], partner).wait_recv()

    def piece(yy, core, q, hh):
        return rp.at[rows(yy), cols((2 * x + core) * W + hh * H + q * CW, CW)]

    for q in range(nq):
        for j, hh in enumerate((oc, c)):
            ref = piece(y, c, q, hh)
            go(remote(ref, ref, yc_send.at[q, j], yc_recv.at[q, j], across), jnp.logical_not(home))

    for d in range(1, nx):
        to = dev(lax.rem(x + d, nx), y, z, c)
        go(remote(mine, mine, xo_send.at[d], xo_recv.at[d], to))

    for hh in range(2):
        src = ksend.at[:, pl.ds(hh * H, H)]
        here = jnp.logical_and(home, c == hh)
        go(
            remote(src, kbuf.at[y], k_send.at[hh], k_recv.at[y], dev(x, c, z, hh)),
            jnp.logical_not(here),
        )

        @pl.when(here)
        def _():
            pltpu.make_async_copy(src, kbuf.at[y], k_recv.at[y]).start()

    tcol = (2 * x + y) * W + c * H

    def yy_of(h):
        return y if h == 0 else oy

    def own_part(q, h):
        return rp.at[rows(yy_of(h)), cols(tcol + q * CW, CW)]

    def slot(zb, q, h):
        return cp.at[zb, rows(yy_of(h)), pl.ds(q * CW, CW)]

    def own_sends(q, h):
        go(
            remote(own_part(q, h), slot(z, q, h), z_send.at[0, z, q, h], z_recv.at[z, q, h], dev(x, y, lax.rem(z + 1, nz), c)),
            z < nz - 1,
        )
        go(
            remote(own_part(q, h), slot(z, q, h), z_send.at[1, z, q, h], z_recv.at[z, q, h], dev(x, y, lax.rem(z + nz - 1, nz), c)),
            z > 0,
        )

    def arrivals(d, q, up):
        zb = lax.rem(z + nz - d, nz) if up else lax.rem(z + d, nz)
        valid = z >= d if up else z + d < nz
        onward = jnp.logical_and(valid, z < nz - 1) if up else jnp.logical_and(valid, z > 0)
        nxt = lax.rem(z + 1, nz) if up else lax.rem(z + nz - 1, nz)
        side = 0 if up else 1
        for h in range(2):
            ref = slot(zb, q, h)
            copy = remote(ref, ref, z_send.at[side, zb, q, h], z_recv.at[zb, q, h], dev(x, y, nxt, c))
            pl.when(valid)(copy.wait_recv)
            go(copy, onward)

    def y_pieces(q):
        for j, hh in enumerate((oc, c)):
            ref = piece(oy, c, q, hh)
            pl.when(home)(remote(ref, ref, yc_send.at[q, j], yc_recv.at[q, j], across).wait_recv)
            go(remote(ref, ref, yf_send.at[q, j], yf_recv.at[q, j], partner), home)

    def y_passed(q, j):
        ref = piece(oy, oc, q, c if j == 0 else oc)
        pl.when(jnp.logical_not(home))(
            remote(ref, ref, yf_send.at[q, j], yf_recv.at[q, j], partner).wait_recv
        )

    ycol_ref = rp.at[rows(oy), cols(mycol, W)]

    def pass_x(cond):
        for d in range(1, nx):
            to = dev(lax.rem(x + d, nx), y, z, c)
            go(remote(ycol_ref, ycol_ref, xd_send.at[d], xd_recv.at[d], to), cond)

    def x_arrive(recv, send, recv2, send2, yy):
        for d in range(1, nx):
            src_x = lax.rem(x + nx - d, nx)
            ref = rp.at[rows(yy), cols((2 * src_x + c) * W, W)]
            remote(ref, ref, send.at[d], recv.at[d], partner).wait_recv()
            go(remote(ref, ref, send2.at[d], recv2.at[d], partner))

    def x_passed(recv2, send2, yy):
        for d in range(1, nx):
            src_x = lax.rem(x + nx - d, nx)
            ref = rp.at[rows(yy), cols((2 * src_x + oc) * W, W)]
            remote(ref, ref, send2.at[d], recv2.at[d], partner).wait_recv()

    low = z < (nz + 1) // 2

    def zb_of(d):
        return jnp.where(low, lax.rem(z + d, nz), lax.rem(z + nz - d, nz))

    def multiply(q, ds):
        for h in range(2):
            part = None
            for d in ds:
                zb = zb_of(d) if d else z
                lhs = rp[pl.ds(h * R, R), pl.ds(mult(zb * 2 * R, 2 * R), 2 * R)]
                if d:
                    rhs = cp[zb, :, pl.ds(q * CW, CW)]
                else:
                    rhs = rp[:, cols(tcol + q * CW, CW)]
                prod = jnp.dot(lhs, rhs, preferred_element_type=jnp.float32)
                part = prod if part is None else part + prod
            where = (pl.ds(h * R, R), pl.ds(q * CW, CW))
            if ds[0]:
                acc[where] = acc[where] + part
            else:
                acc[where] = part

    def inflate(q):
        total = jnp.zeros((1, CW), jnp.float32)
        for h in range(2):
            for i in range(R // TILE):
                where = (pl.ds(h * R + i * TILE, TILE), pl.ds(q * CW, CW))
                value = acc[where]
                value = value * value * kbuf[h, i : i + 1, pl.ds(q * CW, CW)]
                acc[where] = value
                total = total + jnp.sum(value, axis=0, keepdims=True)
        tsend[q] = jnp.broadcast_to(total, (8, CW))
        for d in range(1, nz):
            to = dev(x, y, lax.rem(z + d, nz), c)
            go(remote(tsend.at[q], trecv.at[z, q], t_send.at[d, q], t_recv.at[z, q], to))

    def finish(q):
        total = tsend[q]
        for d in range(1, nz):
            zb = lax.rem(z + d, nz)
            remote(tsend.at[q], trecv.at[zb, q], t_send.at[d, q], t_recv.at[zb, q], partner).wait_recv()
            total = total + trecv[zb, q]
        scale = (order / total)[0:1, :]
        for h in range(2):
            for i in range(R // TILE):
                where = (pl.ds(h * R + i * TILE, TILE), pl.ds(q * CW, CW))
                obuf[where] = (acc[where] * scale).astype(jnp.bfloat16)
        for h in range(2):
            src = obuf.at[pl.ds(h * R, R), pl.ds(q * CW, CW)]
            dst = out.at[:, cols(c * H + q * CW, CW)]
            here = jnp.logical_and(home, y == h)
            go(remote(src, dst, o_send.at[h, q], o_recv.at[c, q], dev(x, h, z, y)), jnp.logical_not(here))

            @pl.when(here)
            def _():
                pltpu.make_async_copy(src, dst, o_recv.at[c, q]).start()

    def panel_ready():
        pa_arrive(1)
        pl.when(home)(functools.partial(pa_arrive, 0))
        for q in range(nq):
            y_passed(q, 1)
        ref = rp.at[rows(oy), cols((2 * x + oc) * W, W)]
        pl.when(home)(remote(ref, ref, yb_send.at[1], yb_recv.at[1], partner).wait_recv)
        x_passed(xf_recv, xf_send, y)
        x_passed(xg_recv, xg_send, oy)
        for h in range(2):
            pltpu.make_async_copy(kbuf.at[h], kbuf.at[h], k_recv.at[h]).wait()

    steps = nq + nz - 2
    done, ahead = 0, None
    for s in range(max(steps, 4)):
        if s < nq:
            if s == 0:
                pl.when(jnp.logical_not(home))(functools.partial(pa_arrive, 0))
            own_sends(s, 0)
            if s == 0:
                y_pieces(0)
            if s == 1:
                for q in range(1, nq):
                    y_pieces(q)
                pass_x(home)
                go(remote(mine, mine, yb_send.at[0], yb_recv.at[0], across), home)
            y_passed(s, 0)
            own_sends(s, 1)
        if s == 2:
            pl.when(jnp.logical_not(home))(
                remote(ycol_ref, ycol_ref, yb_send.at[0], yb_recv.at[0], across).wait_recv
            )
            go(remote(ycol_ref, ycol_ref, yb_send.at[1], yb_recv.at[1], partner), jnp.logical_not(home))
            pass_x(jnp.logical_not(home))
        for d in range(1, nz):
            q = s + 1 - d
            if 0 <= q < nq:
                arrivals(d, q, True)
                arrivals(d, q, False)
        if s == 2:
            x_arrive(xo_recv, xo_send, xf_recv, xf_send, y)
        if s == 3:
            x_arrive(xd_recv, xd_send, xg_recv, xg_send, oy)
            panel_ready()
        ready = [q for q in range(done, nq) if s >= max(q + nz - 2, 3)]
        for q in ready:
            multiply(q, list(range(nz - 1 if q == ahead else 0, nz)))
            inflate(q)
        for q in ready:
            finish(q)
        done += len(ready)
        if s >= 3 and s == nq + nz - 4 and done == nq - 1:
            ahead = done
            multiply(ahead, list(range(nz - 1)))
    for hh in range(2):
        for q in range(nq):
            ref = out.at[:, pl.ds(hh * H + q * CW, CW)]
            pltpu.make_async_copy(ref, ref, o_recv.at[hh, q]).wait()
    for copy, cond in started:
        if cond is None:
            copy.wait_send()
        else:
            pl.when(cond)(copy.wait_send)


def body(similarity, occupancy, kept_tiles):
    R, W = similarity.shape
    nrow, ncol = lax.axis_size("row"), lax.axis_size("col")
    nz, nx = nrow // 2, ncol // 2
    H = W // 2
    nq = H // TILE
    CW = H // nq
    order = R * nrow
    kept_rows = -(-(R // TILE) // 8) * 8
    dma = pltpu.SemaphoreType.DMA
    vmem = pltpu.VMEM
    return pl.pallas_call(
        functools.partial(kernel, nz, nx, nq, float(order)),
        out_shape=jax.ShapeDtypeStruct((R, W), jnp.bfloat16),
        in_specs=[
            pl.BlockSpec(memory_space=pltpu.VMEM),
            pl.BlockSpec(memory_space=pltpu.SMEM),
            pl.BlockSpec(memory_space=pltpu.SMEM),
        ],
        out_specs=pl.BlockSpec(memory_space=pltpu.VMEM),
        scratch_shapes=[
            vmem((2 * R, order), jnp.bfloat16),
            vmem((nz, 2 * R, H), jnp.bfloat16),
            vmem((2 * R, H), jnp.float32),
            vmem((2 * R, H), jnp.bfloat16),
            vmem((nq, 8, CW), jnp.float32),
            vmem((nz, nq, 8, CW), jnp.float32),
            vmem((kept_rows, W), jnp.float32),
            vmem((2, kept_rows, H), jnp.float32),
            dma((2, nz, nq, 2)), dma((nz, nq, 2)),
            dma((2,)), dma((2,)),
            dma((nq, 2)), dma((nq, 2)),
            dma((nq, 2)), dma((nq, 2)),
            dma((2,)), dma((2,)),
            dma((nx,)), dma((nx,)),
            dma((nx,)), dma((nx,)),
            dma((nx,)), dma((nx,)),
            dma((nx,)), dma((nx,)),
            dma((nz, nq)), dma((nz, nq)),
            dma((2, nq)), dma((2, nq)),
            dma((2,)), dma((2,)),
        ],
        compiler_params=pltpu.CompilerParams(
            collective_id=0, has_side_effects=True, vmem_limit_bytes=48 * 2**20
        ),
    )(similarity, occupancy, kept_tiles)


def solution(mesh):
    placed = (P("row", "col"), P("row", "col"), P("row", "col"))
    return jax.shard_map(
        body, mesh=mesh, in_specs=placed, out_specs=P("row", "col"), check_vma=False
    )
```

time: 212 us -> 94.5 us (0.45)
  waiting for transfers between devices: 164 us -> 0 us
  Pallas kernels: 0 us -> 90.8 us
  blocking collectives: 18.4 us -> 0 us
  between operations: 13.5 us -> 0.01 us
  matrix products: 8.14 us -> 0 us
  other arithmetic: 6.76 us -> 0 us
    all_gather x2 -> x0, waiting for transfers between devices: 163 us -> none  [the longest x1 127 us: body(): column_panel = lax.all_gather(stored, 'row', axis=0, tiled=True)]
    pallas_call x0 -> x1, Pallas kernels: none -> 90.8 us  [body(): pl.pallas_call(functools.partial(kernel, nz, nx, nq, float(order)), out_s...]
    psum x1 -> x0, blocking collectives: 18.4 us -> none  [body(): column_total = lax.psum(jnp.sum(inflated, axis=0), 'row')]
    dot_general x1 -> x0, matrix products: 8.14 us -> none  [body(): jnp.dot(lax.all_gather(stored, 'col', axis=1, tiled=True), column_panel,...]
    convert_element_type x3 -> x0, other arithmetic: 2.78 us -> none  [the longest x1 2.09 us: body(): (order * inflated / column_total[None, :]).astype(jnp.bfloat16)]
    mul x1 -> x0, other arithmetic: 2.34 us -> none  [expand_tiles(): masked = shaped * tile_pattern.astype(values.dtype)[:, None, :, None]]
    unnamed x5 -> x7, local copies, waits for them, and re-layouts: 1.27 us -> 3.56 us
  transfers between devices with their start and end apart: 2 -> 0, of which waited for: 2 -> 0; matrix products, arithmetic and copies ran while one was open for 0% -> 0% of each run, Pallas kernels for 0% -> 0%
where the time goes in v1:
time: 94.5 us; the launch traced here: 94.3 us
  Pallas kernels  90.8 us (96%)
  local copies, waits for them, and re-layouts  3.56 us (4%)
    pallas_call x1, Pallas kernels, body(): pl.pallas_call(functools.partial(kernel, nz, nx, nq, float(order)), out_s...  90.8 us
    unnamed x7, local copies, waits for them, and re-layouts  3.56 us

profile of v1, /device:TPU:0, one launch (start us, length us, event | category | flops | bytes accessed | tf_op | source)
XLA Modules:
  0.0 94.3 jit_solution(15333575292699940500)
XLA Ops:
  0.0 0.0 copy-start
  0.0 1.2 %copy-done = bf16[512,1024]{1,0:T(8,128)(2,1)S(1)} copy-done((bf16[512,1024]{1,0:T(8,128)(2,1)S(1)}, bf16[512,1024]{1,0:T(8,128)(2,1)}, u32[]{:S(2)}) %copy-start) | copy-done | bytes 1048600
  1.2 0.0 copy-start.1
  1.2 0.7 copy-done.1
  1.9 0.0 copy-start.2
  1.9 0.7 copy-done.2
  2.6 90.8 %shard_map.37 = bf16[512,1024]{1,0:T(8,128)(2,1)S(1)} custom-call(bf16[512,1024]{1,0:T(8,128)(2,1)S(1)} %copy-done, s32[4,8]{1,0:T(4,128)S(1)} %copy-done.1, s32[4,8]{1,0:T(4,128)S(1)} %copy-done.2), custom_call_target="tpu_custom_call" | custom-call | tf_op jit(solution)/shard_map/pallas_call | solution.py:318
  93.4 1.0 %copy.5 = bf16[512,1024]{1,0:T(8,128)(2,1)} copy(bf16[512,1024]{1,0:T(8,128)(2,1)S(1)} %shard_map.37) | data formatting | bytes 2097152
Async XLA Ops:
  0.0 1.2 %copy-start = (bf16[512,1024]{1,0:T(8,128)(2,1)S(1)}, bf16[512,1024]{1,0:T(8,128)(2,1)}, u32[]{:S(2)}) copy-start(bf16[512,1024]{1,0:T(8,128)(2,1)} %sim.1) | copy-start | bytes 3145732
  1.2 0.7 copy-start.1
  1.9 0.7 copy-start.2

commit v2 on v1

--- a/solution.py
+++ b/solution.py
@@ -13,11 +13,11 @@
 
 def kernel(
     nz, nx, nq, order,
-    sim, occ, kept, out,
-    rp, cp, acc, obuf, tsend, trecv, ksend, kbuf,
+    sim_any, occ_any, kept_any, out,
+    sim, occ, kept, rp, cp, acc, obuf, tsend, trecv, ksend, kbuf,
     z_send, z_recv, pa_send, pa_recv, yc_send, yc_recv, yf_send, yf_recv,
     yb_send, yb_recv, xo_send, xo_recv, xf_send, xf_recv, xd_send, xd_recv, xg_send, xg_recv,
-    t_send, t_recv, o_send, o_recv, k_send, k_recv,
+    t_send, t_recv, o_send, o_recv, k_send, k_recv, in_sem,
 ):
     R, W = sim.shape
     H = W // 2
@@ -63,10 +63,19 @@
     for peer in peers:
         pl.semaphore_signal(barrier, inc=1, device_id=peer, device_id_type=MESH)
 
+    loads = [
+        pltpu.make_async_copy(src, dst, in_sem.at[i])
+        for i, (src, dst) in enumerate(((sim_any, sim), (occ_any, occ), (kept_any, kept)))
+    ]
+    for load in loads:
+        load.start()
+    for load in loads:
+        load.wait()
+
     mycol = (2 * x + c) * W
     for i in range(R // TILE):
         for j in range(W // TILE):
-            flag = occ[i, j].astype(jnp.float32)
+            flag = occ[i : i + 1, j : j + 1].astype(jnp.float32)
             tile = sim[i * TILE : (i + 1) * TILE, j * TILE : (j + 1) * TILE].astype(jnp.float32)
             rp[pl.ds(mult(y * R + i * TILE, TILE), TILE), cols(mycol + j * TILE, TILE)] = (tile * flag).astype(
                 jnp.bfloat16
@@ -74,8 +83,8 @@
     ksend[...] = jnp.zeros_like(ksend)
     for i in range(R // TILE):
         for j in range(W // TILE):
-            ksend[i : i + 1, j * TILE : (j + 1) * TILE] = jnp.full(
-                (1, TILE), kept[i, j].astype(jnp.float32), jnp.float32
+            ksend[i : i + 1, j * TILE : (j + 1) * TILE] = jnp.broadcast_to(
+                kept[i : i + 1, j : j + 1].astype(jnp.float32), (1, TILE)
             )
     pl.semaphore_wait(barrier, len(peers))
 
@@ -251,48 +260,38 @@
         for h in range(2):
             pltpu.make_async_copy(kbuf.at[h], kbuf.at[h], k_recv.at[h]).wait()
 
-    steps = nq + nz - 2
-    done, ahead = 0, None
-    for s in range(max(steps, 4)):
-        if s < nq:
-            if s == 0:
-                pl.when(jnp.logical_not(home))(functools.partial(pa_arrive, 0))
-            own_sends(s, 0)
-            if s == 0:
-                y_pieces(0)
-            if s == 1:
-                for q in range(1, nq):
-                    y_pieces(q)
-                pass_x(home)
-                go(remote(mine, mine, yb_send.at[0], yb_recv.at[0], across), home)
-            y_passed(s, 0)
-            own_sends(s, 1)
-        if s == 2:
+    pl.when(jnp.logical_not(home))(functools.partial(pa_arrive, 0))
+    for q in range(nq):
+        own_sends(q, 0)
+    for q in range(nq):
+        y_pieces(q)
+        y_passed(q, 0)
+        own_sends(q, 1)
+    pass_x(home)
+    go(remote(mine, mine, yb_send.at[0], yb_recv.at[0], across), home)
+    for d in range(1, nz - 1):
+        for q in range(nq):
+            arrivals(d, q, True)
+            arrivals(d, q, False)
+        if d == 1:
             pl.when(jnp.logical_not(home))(
                 remote(ycol_ref, ycol_ref, yb_send.at[0], yb_recv.at[0], across).wait_recv
             )
             go(remote(ycol_ref, ycol_ref, yb_send.at[1], yb_recv.at[1], partner), jnp.logical_not(home))
             pass_x(jnp.logical_not(home))
-        for d in range(1, nz):
-            q = s + 1 - d
-            if 0 <= q < nq:
-                arrivals(d, q, True)
-                arrivals(d, q, False)
-        if s == 2:
             x_arrive(xo_recv, xo_send, xf_recv, xf_send, y)
-        if s == 3:
-            x_arrive(xd_recv, xd_send, xg_recv, xg_send, oy)
-            panel_ready()
-        ready = [q for q in range(done, nq) if s >= max(q + nz - 2, 3)]
-        for q in ready:
-            multiply(q, list(range(nz - 1 if q == ahead else 0, nz)))
-            inflate(q)
-        for q in ready:
-            finish(q)
-        done += len(ready)
-        if s >= 3 and s == nq + nz - 4 and done == nq - 1:
-            ahead = done
-            multiply(ahead, list(range(nz - 1)))
+    x_arrive(xd_recv, xd_send, xg_recv, xg_send, oy)
+    panel_ready()
+    for q in range(nq):
+        multiply(q, list(range(nz - 1)))
+    for q in range(nq):
+        arrivals(nz - 1, q, True)
+        arrivals(nz - 1, q, False)
+        multiply(q, [nz - 1])
+        inflate(q)
+        if q:
+            finish(q - 1)
+    finish(nq - 1)
     for hh in range(2):
         for q in range(nq):
             ref = out.at[:, pl.ds(hh * H + q * CW, CW)]
@@ -318,13 +317,12 @@
     return pl.pallas_call(
         functools.partial(kernel, nz, nx, nq, float(order)),
         out_shape=jax.ShapeDtypeStruct((R, W), jnp.bfloat16),
-        in_specs=[
-            pl.BlockSpec(memory_space=pltpu.VMEM),
-            pl.BlockSpec(memory_space=pltpu.SMEM),
-            pl.BlockSpec(memory_space=pltpu.SMEM),
-        ],
-        out_specs=pl.BlockSpec(memory_space=pltpu.VMEM),
+        in_specs=[pl.BlockSpec(memory_space=pltpu.HBM)] * 3,
+        out_specs=pl.BlockSpec(memory_space=pltpu.HBM),
         scratch_shapes=[
+            vmem((R, W), jnp.bfloat16),
+            vmem(occupancy.shape, jnp.int32),
+            vmem(kept_tiles.shape, jnp.int32),
             vmem((2 * R, order), jnp.bfloat16),
             vmem((nz, 2 * R, H), jnp.bfloat16),
             vmem((2 * R, H), jnp.float32),
@@ -345,9 +343,10 @@
             dma((nz, nq)), dma((nz, nq)),
             dma((2, nq)), dma((2, nq)),
             dma((2,)), dma((2,)),
+            dma((3,)),
         ],
         compiler_params=pltpu.CompilerParams(
-            collective_id=0, has_side_effects=True, vmem_limit_bytes=48 * 2**20
+            collective_id=0, has_side_effects=True, vmem_limit_bytes=63 * 2**20
         ),
     )(similarity, occupancy, kept_tiles)
 

time: 94.5 us -> 90.4 us (0.957)
  Pallas kernels: 90.8 us -> 87.8 us
  local copies, waits for them, and re-layouts: 3.56 us -> 2.26 us
    pallas_call x1, Pallas kernels: 90.8 us -> 87.8 us  [body(): pl.pallas_call(functools.partial(kernel, nz, nx, nq, float(order)), out_s...]
    unnamed x7 -> x1, local copies, waits for them, and re-layouts: 3.56 us -> 2.26 us
where the time goes in v2:
time: 90.4 us; the launch traced here: 90 us
  Pallas kernels  87.8 us (97%)
  local copies, waits for them, and re-layouts  2.26 us (2%)
    pallas_call x1, Pallas kernels, body(): pl.pallas_call(functools.partial(kernel, nz, nx, nq, float(order)), out_s...  87.8 us
    unnamed x1, local copies, waits for them, and re-layouts  2.26 us

profile of v2, /device:TPU:0, one launch (start us, length us, event | category | flops | bytes accessed | tf_op | source)
XLA Modules:
  0.0 90.0 jit_solution(1032891636471204625)
XLA Ops:
  0.0 87.8 %shard_map.37 = bf16[512,1024]{1,0:T(8,128)(2,1)} custom-call(bf16[512,1024]{1,0:T(8,128)(2,1)} %sim_any.1, s32[4,8]{1,0:T(4,128)} %occ_any.1, s32[4,8]{1,0:T(4,128)} %kept_any.1), custom_call_target="tpu_custom_call" | custom-call | tf_op jit(solution)/shard_map/pallas_call | solution.py:317
  87.8 2.3 %copy.5 = bf16[512,1024]{1,0:T(8,128)(2,1)} copy(bf16[512,1024]{1,0:T(8,128)(2,1)} %shard_map.37) | data formatting | bytes 2097152
